TPU v7x, 32 devices: a whole 2x2x4 slice. The times are simulated.
32 devices in a mesh: groups: 2 (over x), blk: 8 (over z, y), atoms: 2 (over core).
Axes of the slice: x: 2, y: 2, z: 4, core: 2. Of those that a mesh axis runs over, the one named last changes fastest.
Arguments:
- density: bfloat16 [384, 1024], P('groups', 'blk'), parts along dimension 0, may hold values from -6 to 6
- three_centre: bfloat16 [16, 2, 4, 128, 2048], P(('groups', 'blk'), 'atoms'), parts along dimension 0, may hold values from -0.0078125 to 0.0078125
- pattern: int32 [16, 2, 4], P(('groups', 'blk'), 'atoms'), parts along dimension 0, may hold values from 0 to 7, all different within a row
- domain: int32 [16, 2, 2], P(('groups', 'blk')), parts along dimension 0, may hold values from 0 to 1
- owner: int32 [16, 2], P(('groups', 'blk')), parts along dimension 0, may hold values from 0 to 1, each once within a row
- metric: bfloat16 [16, 2, 1024, 1024], P(('groups', 'blk'), 'atoms'), parts along dimension 0, may hold values from -1 to 3, as said below
Outputs:
- exchange: float32 [16, 2, 192, 192], P(('groups', 'blk'), 'atoms'), parts along dimension 0
There are 2 independent parts, one for each index of `groups`. A program takes and returns all parts, laid end to end along the dimension named above; each array names one. Nothing has to cross between parts.
Inputs may be any that keep to these rules, and one draw needn't show every extreme that they name: `pattern`: each device's entries are different tiles. `owner`: each row is an order of the atom groups. `metric`: each matrix is symmetric with a positive diagonal.
All inputs are finite; a program needn't handle non-finite values.
Results may differ from a plain program's by a relative error of at most 0.0013.
Values may be sent and summed in bfloat16 or wider, within the bound.
No kernel may reach another device: no remote copies, remote signals or barrier semaphores. Data moves between devices by JAX's collectives and lax.ppermute only.
A program may use at most 64 MiB of HBM per device.

v0:
```python
import functools
import jax
import jax.numpy as jnp
from jax import lax
from jax.experimental import pallas as pl
from jax.experimental.pallas import tpu as pltpu
from jax.sharding import PartitionSpec as P

AXES = ("blk", "atoms")
TRANSPOSED = (((1,), (1,)), ((), ()))
BLOCK = 256


def between_blocks(block, even, odd):
    pairs = []
    for targets, core in ((even, 0), (odd, 1)):
        pairs += [(2 * b + core, 2 * target + core) for b, target in enumerate(targets)]
    return lax.ppermute(block, AXES, pairs)


def swap_cores(block):
    return lax.ppermute(block, "atoms", [(0, 1), (1, 0)])


def far(array):
    return pltpu.with_memory_space_constraint(array, pltpu.HBM)


EIGHT = (
    ((3, 4, 5, 2, 1, 6, 7, 0), (4, 3, 6, 7, 2, 1, 0, 5), (1, 0, 3, 5, 6, 7, 2, 4), (2, 5, 0, 1, 7, 3, 4, 6)),
    ((6, 2, 7, 4, 5, 0, 1, 3), (5, 7, 4, 6, 0, 2, 3, 1), (7, 6, 1, 0, 3, 4, 5, 2), (1, 0, 3, 2, 5, 4, 7, 6)),
)


def routes(count):
    if count == 8:
        return list(zip(*EIGHT))
    offsets = list(range(count - 1, 0, -1))
    steps = []
    for k in range(0, count - 1, 2):
        even = tuple((b + offsets[k]) % count for b in range(count))
        odd = tuple((b + offsets[k + 1]) % count for b in range(count)) if k + 1 < len(offsets) else ()
        steps.append((even, odd))
    return steps


def origin_of(targets, count, block):
    if not targets:
        return jnp.int32(count)
    origin = jnp.int32(0)
    for b, target in enumerate(targets):
        origin = jnp.where(block == target, b, origin)
    return origin


def stage_kernel(*refs):
    (density, centre, metric), indices_far = refs[:3], refs[3:6]
    own, rows, matrix, message, control = refs[6:11]
    indices, sem = refs[11:14], refs[14]
    pattern, domain, owner = indices
    copies = [pltpu.make_async_copy(away, near, sem.at[i]) for i, (away, near) in enumerate(zip(indices_far, indices))]
    loads = [
        pltpu.make_async_copy(density, own, sem.at[3]),
        pltpu.make_async_copy(centre.at[0, 0], rows, sem.at[4]),
        pltpu.make_async_copy(metric.at[0, 0], matrix, sem.at[5]),
    ]
    for copy in copies + loads:
        copy.start()
    for copy in copies:
        copy.wait()
    core = lax.axis_index("atoms")
    segs, slots = domain.shape[2], pattern.shape[2]
    line = lax.broadcasted_iota(jnp.int32, message.shape, 0)
    chosen = jnp.zeros(message.shape, jnp.int32)
    for slot in range(slots):
        chosen = jnp.where(line == slot, pattern[0, 0, slot], chosen)
    message[...] = chosen.astype(jnp.float32).astype(message.dtype)
    line = lax.broadcasted_iota(jnp.int32, control.shape, 0)
    mine = jnp.zeros(control.shape, jnp.int32)
    for source in range(2):
        origin = core if source == 0 else 1 - core
        for seg in range(segs):
            target = owner[0, domain[0, origin, seg]]
            mine = jnp.where(line == source * segs + seg, jnp.where(target == core, 1, 0), mine)
    control[...] = mine
    for load in loads:
        load.wait()


def exchange_kernel(plan, count, own, packed, swapped, message, control, rows, rows_other, matrix, out, table, dens, total_ref):
    block = lax.axis_index("blk")
    core = lax.axis_index("atoms")
    slots, width = rows.shape[0], rows.shape[1]
    aux = matrix.shape[1]
    segs = rows.shape[2] // aux
    nocc = dens.shape[1]
    end = nocc * len(plan)

    def slot_numbers(lines):
        values = lines.astype(jnp.float32)
        return [jnp.max(values[slot : slot + 1]).astype(jnp.int32) for slot in range(slots)]

    chosen_by = [slot_numbers(message[...]), slot_numbers(swapped[end:])]
    table[block] = own[...]
    for step, targets in enumerate(plan):
        origins = [origin_of(side, count, block) for side in targets]
        span = slice(step * nocc, (step + 1) * nocc)
        table[jnp.where(core == 0, origins[0], origins[1])] = packed[span]
        table[jnp.where(core == 0, origins[1], origins[0])] = swapped[span]
    for source, chosen in enumerate(chosen_by):
        for slot in range(slots):
            dens[source, :, slot * width : (slot + 1) * width] = table[chosen[slot]]
    flags = control[...].astype(jnp.float32)
    targeted = [jnp.max(flags[i : i + 1]) > 0.5 for i in range(2 * segs)]

    def halves(source, first, number):
        centre = (rows, rows_other.at[0, 0])[source]
        wide = centre[:, :, first * aux : (first + number) * aux].reshape(slots * width, number * aux)
        return jnp.dot(dens[source], wide, preferred_element_type=jnp.float32).astype(jnp.bfloat16)

    def lower_product(parts):
        total = jnp.zeros((nocc, nocc), jnp.float32)
        stack = jnp.concatenate(parts, 0)
        columns = [0.0] * (aux // BLOCK)
        for i in range(aux // BLOCK):
            lines = slice(i * BLOCK, (i + 1) * BLOCK)
            wide = jnp.dot(stack[:, lines], matrix[lines, i * BLOCK :], preferred_element_type=jnp.float32)
            for j in range(i, aux // BLOCK):
                piece = wide[:, (j - i) * BLOCK : (j - i + 1) * BLOCK]
                columns[j] += 0.5 * piece if i == j else piece
        for i, column in enumerate(columns):
            fitted = column.astype(jnp.bfloat16)
            for seg, part in enumerate(parts):
                total += lax.dot_general(
                    fitted[seg * nocc : (seg + 1) * nocc], part[:, i * BLOCK : (i + 1) * BLOCK], TRANSPOSED,
                    preferred_element_type=jnp.float32,
                )
        return total

    total_ref[...] = jnp.zeros_like(total_ref)
    for source in range(2):
        mine = targeted[source * segs : (source + 1) * segs]
        every = functools.reduce(jnp.logical_and, mine)

        @pl.when(every)
        def _():
            half = halves(source, 0, segs)
            total_ref[...] += lower_product([half[:, seg * aux : (seg + 1) * aux] for seg in range(segs)])

        for seg in range(segs):

            @pl.when(mine[seg] & ~every)
            def _():
                total_ref[...] += lower_product([halves(source, seg, 1)])

    out[0, 0] = total_ref[...] + total_ref[...].T


def local(count, density, three_centre, pattern, domain, owner, metric):
    nocc = density.shape[0]
    slots, width = three_centre.shape[2:4]
    segs = domain.shape[2]
    plan = routes(count)
    received = [between_blocks(density, even, odd) for even, odd in plan]
    centre_other = swap_cores(three_centre)
    vmem = pl.BlockSpec(memory_space=pltpu.VMEM)
    hbm = pl.BlockSpec(memory_space=pltpu.HBM)
    limit = 24 * 1024 * 1024
    lines = -(-slots // 16) * 16
    own, rows, matrix, message, control = pl.pallas_call(
        stage_kernel,
        out_shape=(
            jax.ShapeDtypeStruct(density.shape, density.dtype),
            jax.ShapeDtypeStruct(three_centre.shape[2:], three_centre.dtype),
            jax.ShapeDtypeStruct(metric.shape[2:], metric.dtype),
            jax.ShapeDtypeStruct((lines, width), density.dtype),
            jax.ShapeDtypeStruct((-(-2 * segs // 8) * 8, 128), jnp.int32),
        ),
        in_specs=[hbm] * 6,
        out_specs=[vmem] * 5,
        scratch_shapes=[
            pltpu.SMEM(pattern.shape, jnp.int32),
            pltpu.SMEM(domain.shape, jnp.int32),
            pltpu.SMEM(owner.shape, jnp.int32),
            pltpu.SemaphoreType.DMA((6,)),
        ],
        compiler_params=pltpu.CompilerParams(vmem_limit_bytes=limit),
    )(*[far(array) for array in (density, three_centre, metric, pattern, domain, owner)])
    for k in range(len(received)):
        received[k], message = lax.optimization_barrier((received[k], message))
    packed = jnp.concatenate(received + [message], 0)
    swapped = swap_cores(packed)
    return pl.pallas_call(
        functools.partial(exchange_kernel, plan, count),
        out_shape=jax.ShapeDtypeStruct((1, 1, nocc, nocc), jnp.float32),
        in_specs=[vmem] * 8,
        out_specs=vmem,
        scratch_shapes=[
            pltpu.VMEM((count + 1, nocc, width), jnp.bfloat16),
            pltpu.VMEM((2, nocc, slots * width), jnp.bfloat16),
            pltpu.VMEM((nocc, nocc), jnp.float32),
        ],
        compiler_params=pltpu.CompilerParams(vmem_limit_bytes=limit),
    )(own, packed, swapped, message, control, rows, centre_other, matrix)


def solution(mesh):
    in_specs = (
        P("groups", "blk"),
        P(("groups", "blk"), "atoms", None, None, None),
        P(("groups", "blk"), "atoms", None),
        P(("groups", "blk"), None, None),
        P(("groups", "blk"), None),
        P(("groups", "blk"), "atoms", None, None),
    )
    out_specs = P(("groups", "blk"), "atoms", None, None)
    body = functools.partial(local, mesh.shape["blk"])
    return jax.shard_map(body, mesh=mesh, in_specs=in_specs, out_specs=out_specs, check_vma=False)
```

profile of v0, /device:TPU:1, one launch (start us, length us, event | category | flops | bytes accessed | tf_op | source)
XLA Modules:
  0.0 16.3 jit_solution(6593713531247143495)
XLA Ops:
  0.0 0.1 collective-permute-start.5
  0.1 4.8 %collective-permute-start = (bf16[192,128]{1,0:T(8,128)(2,1)}, bf16[192,128]{1,0:T(8,128)(2,1)S(1)}, u32[]{:S(2)}, u32[]{:S(2)}) collective-permute-start(bf16[192,128]{1,0:T(8,128)(2,1)} %refs_0_.1), channel_id=1, source_target_pairs={{0,6},{2,8},{4,10},{6,4},{8,2},{10,12},{12,14},{14,0},{1,13},{3,5}... | collective-permute-start | bytes 147464 | tf_op jit(solution)/shard_map/ppermute | solution.py:18
  4.8 0.0 collective-permute-start.1
  4.8 2.1 %collective-permute-start.2 = (bf16[192,128]{1,0:T(8,128)(2,1)}, bf16[192,128]{1,0:T(8,128)(2,1)S(1)}, u32[]{:S(2)}, u32[]{:S(2)}) collective-permute-start(bf16[192,128]{1,0:T(8,128)(2,1)} %refs_0_.1), channel_id=1, source_target_pairs={{0,2},{2,0},{4,6},{6,10},{8,12},{10,14},{12,4},{14,8},{1,15},{3,13... | collective-permute-start | bytes 147464 | tf_op jit(solution)/shard_map/ppermute | solution.py:18
  7.0 1.3 %collective-permute-start.3 = (bf16[192,128]{1,0:T(8,128)(2,1)}, bf16[192,128]{1,0:T(8,128)(2,1)S(1)}, u32[]{:S(2)}, u32[]{:S(2)}) collective-permute-start(bf16[192,128]{1,0:T(8,128)(2,1)} %refs_0_.1), channel_id=1, source_target_pairs={{0,4},{2,10},{4,0},{6,2},{8,14},{10,6},{12,8},{14,12},{1,3},{3,1},... | collective-permute-start | bytes 147464 | tf_op jit(solution)/shard_map/ppermute | solution.py:18
  8.3 2.3 %shard_map.64 = (bf16[192,128]{1,0:T(8,128)(2,1)S(1)}, bf16[4,128,2048]{2,1,0:T(8,128)(2,1)S(1)}, bf16[1024,1024]{1,0:T(8,128)(2,1)S(1)}, bf16[16,128]{1,0:T(8,128)(2,1)S(1)}, s32[8,128]{1,0:T(8,128)S(1)}) custom-call(bf16[192,128]{1,0:T(8,128)(2,1)} %refs_0_.1, bf16[1,1,4,128,2048]{4,3,2,1,0:T(8,128)(2,1)} %refs_1_.1, bf16[1,1,1024,1024]{3,2,1,0:T(8,128)(2,1)} %refs_2_.1, ...), custom_call_target="tpu_custom_call" | custom-call | tf_op jit(solution)/shard_map/pallas_call | solution.py:170
  10.6 0.0 collective-permute-done
  10.6 0.0 collective-permute-done.1
  10.6 0.0 collective-permute-done.2
  10.6 0.0 collective-permute-done.3
  10.7 0.7 %collective-permute-start.4 = (bf16[784,128]{1,0:T(8,128)(2,1)S(1)}, bf16[784,128]{1,0:T(8,128)(2,1)S(1)}, u32[]{:S(2)}, u32[]{:S(2)}) collective-permute-start(bf16[784,128]{1,0:T(8,128)(2,1)S(1)} %constant_dynamic-update-slice_fusion.packed), channel_id=1, source_target_pairs={{0,1},{1,0},{2,3},{3,2},{4,5},{5,4},{6,7},{7,6},{8,9},{9,8},{10,11... | collective-permute-start | bytes 602120 | tf_op jit(solution)/shard_map/ppermute | solution.py:22
  11.4 1.1 %collective-permute-done.4.swapped = bf16[784,128]{1,0:T(8,128)(2,1)S(1)} collective-permute-done((bf16[784,128]{1,0:T(8,128)(2,1)S(1)}, bf16[784,128]{1,0:T(8,128)(2,1)S(1)}, u32[]{:S(2)}, u32[]{:S(2)}) %collective-permute-start.4) | collective-permute-done | bytes 200736 | tf_op jit(solution)/shard_map/ppermute | solution.py:22
  12.5 0.0 collective-permute-done.5.rows_other
  12.5 3.9 %shard_map.65 = f32[1,1,192,192]{3,2,1,0:T(8,128)} custom-call(bf16[192,128]{1,0:T(8,128)(2,1)S(1)} %get-tuple-element.18.own, bf16[784,128]{1,0:T(8,128)(2,1)S(1)} %constant_dynamic-update-slice_fusion.packed, bf16[784,128]{1,0:T(8,128)(2,1)S(1)} %collective-permute-done.4.swapped, bf16[16,128]{1,0:T(8,128)(2,1)S(1)} %get-tuple-element.27.message, ...), custom_call_target="tpu_custom_call" | custom-call | tf_op jit(solution)/shard_map/pallas_call | solution.py:193
  (5 shorter events, 0.0 us)
Async XLA Ops:
  0.0 12.5 %collective-permute-start.5 = (bf16[1,1,4,128,2048]{4,3,2,1,0:T(8,128)(2,1)}, bf16[1,1,4,128,2048]{4,3,2,1,0:T(8,128)(2,1)S(1)}, u32[]{:S(2)}, u32[]{:S(2)}) collective-permute-start(bf16[1,1,4,128,2048]{4,3,2,1,0:T(8,128)(2,1)} %refs_1_.1), channel_id=1, source_target_pairs={{0,1},{1,0},{2,3},{3,2},{4,5},{5,4},{6,7},{7,6},{8,9},{9,8},{10,11... | collective-permute-start | bytes 6291464 | tf_op jit(solution)/shard_map/ppermute | solution.py:22
  0.1 10.5 %collective-permute-start = (bf16[192,128]{1,0:T(8,128)(2,1)}, bf16[192,128]{1,0:T(8,128)(2,1)S(1)}, u32[]{:S(2)}, u32[]{:S(2)}) collective-permute-start(bf16[192,128]{1,0:T(8,128)(2,1)} %refs_0_.1), channel_id=1, source_target_pairs={{0,6},{2,8},{4,10},{6,4},{8,2},{10,12},{12,14},{14,0},{1,13},{3,5}... | collective-permute-start | bytes 147464 | tf_op jit(solution)/shard_map/ppermute | solution.py:18
  4.8 5.8 %collective-permute-start.1 = (bf16[192,128]{1,0:T(8,128)(2,1)}, bf16[192,128]{1,0:T(8,128)(2,1)S(1)}, u32[]{:S(2)}, u32[]{:S(2)}) collective-permute-start(bf16[192,128]{1,0:T(8,128)(2,1)} %refs_0_.1), channel_id=1, source_target_pairs={{0,8},{2,6},{4,12},{6,14},{8,4},{10,2},{12,0},{14,10},{1,11},{3,15... | collective-permute-start | bytes 147464 | tf_op jit(solution)/shard_map/ppermute | solution.py:18
  4.8 5.8 %collective-permute-start.2 = (bf16[192,128]{1,0:T(8,128)(2,1)}, bf16[192,128]{1,0:T(8,128)(2,1)S(1)}, u32[]{:S(2)}, u32[]{:S(2)}) collective-permute-start(bf16[192,128]{1,0:T(8,128)(2,1)} %refs_0_.1), channel_id=1, source_target_pairs={{0,2},{2,0},{4,6},{6,10},{8,12},{10,14},{12,4},{14,8},{1,15},{3,13... | collective-permute-start | bytes 147464 | tf_op jit(solution)/shard_map/ppermute | solution.py:18
  7.0 3.6 %collective-permute-start.3 = (bf16[192,128]{1,0:T(8,128)(2,1)}, bf16[192,128]{1,0:T(8,128)(2,1)S(1)}, u32[]{:S(2)}, u32[]{:S(2)}) collective-permute-start(bf16[192,128]{1,0:T(8,128)(2,1)} %refs_0_.1), channel_id=1, source_target_pairs={{0,4},{2,10},{4,0},{6,2},{8,14},{10,6},{12,8},{14,12},{1,3},{3,1},... | collective-permute-start | bytes 147464 | tf_op jit(solution)/shard_map/ppermute | solution.py:18
  10.7 1.8 %collective-permute-start.4 = (bf16[784,128]{1,0:T(8,128)(2,1)S(1)}, bf16[784,128]{1,0:T(8,128)(2,1)S(1)}, u32[]{:S(2)}, u32[]{:S(2)}) collective-permute-start(bf16[784,128]{1,0:T(8,128)(2,1)S(1)} %constant_dynamic-update-slice_fusion.packed), channel_id=1, source_target_pairs={{0,1},{1,0},{2,3},{3,2},{4,5},{5,4},{6,7},{7,6},{8,9},{9,8},{10,11... | collective-permute-start | bytes 602120 | tf_op jit(solution)/shard_map/ppermute | solution.py:22
where the time goes:
time: 16.1 us; the launch traced here: 16.3 us
  starting transfers between devices  8.95 us (56%)
  Pallas kernels  6.17 us (38%)
  waiting for transfers between devices  1.09 us (7%)
    ppermute x4, starting transfers between devices, between_blocks(): return lax.ppermute(block, AXES, pairs)  8.2 us
    pallas_call x1, Pallas kernels, local(): pl.pallas_call(functools.partial(exchange_kernel, plan, count), out_shape...  3.87 us
    pallas_call x1, Pallas kernels, local(): pl.pallas_call(stage_kernel, out_shape=(jax.ShapeDtypeStruct(density.shap...  2.3 us
    ppermute x2, waiting for transfers between devices, swap_cores(): return lax.ppermute(block, 'atoms', [(0, 1), (1, 0)])  1.08 us
    ppermute x2, starting transfers between devices, swap_cores(): return lax.ppermute(block, 'atoms', [(0, 1), (1, 0)])  0.75 us
  transfers between devices with their start and end apart: 6, of which 1 were waited for; matrix products, arithmetic and copies ran while one was open for 0% of the time, Pallas kernels for 14%

commit v1 on v0

--- a/solution.py
+++ b/solution.py
@@ -27,26 +27,21 @@
 
 
 EIGHT = (
-    ((3, 4, 5, 2, 1, 6, 7, 0), (4, 3, 6, 7, 2, 1, 0, 5), (1, 0, 3, 5, 6, 7, 2, 4), (2, 5, 0, 1, 7, 3, 4, 6)),
-    ((6, 2, 7, 4, 5, 0, 1, 3), (5, 7, 4, 6, 0, 2, 3, 1), (7, 6, 1, 0, 3, 4, 5, 2), (1, 0, 3, 2, 5, 4, 7, 6)),
+    ((1, 3, 6, 5, 2, 7, 4, 0), (4, 7, 5, 0, 6, 3, 1, 2), (5, 6, 4, 7, 3, 0, 2, 1), (2, 0, 3, 1, 5, 4, 7, 6)),
+    ((3, 5, 1, 6, 7, 2, 0, 4), (6, 2, 7, 4, 0, 1, 3, 5), (7, 4, 0, 2, 1, 6, 5, 3), (2, 0, 3, 1, 5, 4, 7, 6)),
 )
 
 
 def routes(count):
     if count == 8:
-        return list(zip(*EIGHT))
-    offsets = list(range(count - 1, 0, -1))
-    steps = []
-    for k in range(0, count - 1, 2):
-        even = tuple((b + offsets[k]) % count for b in range(count))
-        odd = tuple((b + offsets[k + 1]) % count for b in range(count)) if k + 1 < len(offsets) else ()
-        steps.append((even, odd))
-    return steps
+        return list(zip(EIGHT[0][:3], EIGHT[1][:3])), EIGHT[0][3]
+    shifts = [tuple((b + k) % count for b in range(count)) for k in range(count - 1, 1, -1)]
+    shared = tuple((b + 1) % count for b in range(count))
+    shifts += [shared] * (len(shifts) % 2)
+    return list(zip(shifts[::2], shifts[1::2])), shared
 
 
 def origin_of(targets, count, block):
-    if not targets:
-        return jnp.int32(count)
     origin = jnp.int32(0)
     for b, target in enumerate(targets):
         origin = jnp.where(block == target, b, origin)
@@ -87,7 +82,11 @@
         load.wait()
 
 
-def exchange_kernel(plan, count, own, packed, swapped, message, control, rows, rows_other, matrix, out, table, dens, total_ref):
+def hold_kernel(given, taken):
+    taken[...] = given[...]
+
+
+def exchange_kernel(plan, shared, count, own, last, packed, swapped, message, control, rows, rows_other, matrix, out, table, dens, total_ref):
     block = lax.axis_index("blk")
     core = lax.axis_index("atoms")
     slots, width = rows.shape[0], rows.shape[1]
@@ -102,11 +101,12 @@
 
     chosen_by = [slot_numbers(message[...]), slot_numbers(swapped[end:])]
     table[block] = own[...]
-    for step, targets in enumerate(plan):
-        origins = [origin_of(side, count, block) for side in targets]
+    for step, (even, odd) in enumerate(plan):
+        near, across = origin_of(even, count, block), origin_of(odd, count, block)
         span = slice(step * nocc, (step + 1) * nocc)
-        table[jnp.where(core == 0, origins[0], origins[1])] = packed[span]
-        table[jnp.where(core == 0, origins[1], origins[0])] = swapped[span]
+        table[jnp.where(core == 0, near, across)] = packed[span]
+        table[jnp.where(core == 0, across, near)] = swapped[span]
+    table[origin_of(shared, count, block)] = last[...]
     for source, chosen in enumerate(chosen_by):
         for slot in range(slots):
             dens[source, :, slot * width : (slot + 1) * width] = table[chosen[slot]]
@@ -160,8 +160,9 @@
     nocc = density.shape[0]
     slots, width = three_centre.shape[2:4]
     segs = domain.shape[2]
-    plan = routes(count)
+    plan, shared = routes(count)
     received = [between_blocks(density, even, odd) for even, odd in plan]
+    last = between_blocks(density, shared, shared)
     centre_other = swap_cores(three_centre)
     vmem = pl.BlockSpec(memory_space=pltpu.VMEM)
     hbm = pl.BlockSpec(memory_space=pltpu.HBM)
@@ -188,20 +189,29 @@
     )(*[far(array) for array in (density, three_centre, metric, pattern, domain, owner)])
     for k in range(len(received)):
         received[k], message = lax.optimization_barrier((received[k], message))
+    last, _ = lax.optimization_barrier((last, message))
+    last = pl.pallas_call(
+        hold_kernel,
+        out_shape=jax.ShapeDtypeStruct(last.shape, last.dtype),
+        in_specs=[vmem],
+        out_specs=vmem,
+        compiler_params=pltpu.CompilerParams(vmem_limit_bytes=limit),
+        cost_estimate=pl.CostEstimate(flops=1400000000, bytes_accessed=2 * last.size * 2, transcendentals=0),
+    )(last)
     packed = jnp.concatenate(received + [message], 0)
     swapped = swap_cores(packed)
     return pl.pallas_call(
-        functools.partial(exchange_kernel, plan, count),
+        functools.partial(exchange_kernel, plan, shared, count),
         out_shape=jax.ShapeDtypeStruct((1, 1, nocc, nocc), jnp.float32),
-        in_specs=[vmem] * 8,
+        in_specs=[vmem] * 9,
         out_specs=vmem,
         scratch_shapes=[
-            pltpu.VMEM((count + 1, nocc, width), jnp.bfloat16),
+            pltpu.VMEM((count, nocc, width), jnp.bfloat16),
             pltpu.VMEM((2, nocc, slots * width), jnp.bfloat16),
             pltpu.VMEM((nocc, nocc), jnp.float32),
         ],
         compiler_params=pltpu.CompilerParams(vmem_limit_bytes=limit),
-    )(own, packed, swapped, message, control, rows, centre_other, matrix)
+    )(own, last, packed, swapped, message, control, rows, centre_other, matrix)
 
 
 def solution(mesh):

time: 16.1 us -> 15.1 us (0.938); the launches traced: 16.3 us -> 15.1 us
  starting transfers between devices: 8.95 us -> 8.38 us
  Pallas kernels: 6.17 us -> 5.61 us
    ppermute x4, starting transfers between devices: 8.2 us -> 6.24 us  [between_blocks(): return lax.ppermute(block, AXES, pairs)]
    ppermute x2, starting transfers between devices: 0.75 us -> 2.15 us  [swap_cores(): return lax.ppermute(block, 'atoms', [(0, 1), (1, 0)])]
    pallas_call x1 -> x2, Pallas kernels: 3.87 us -> 3.31 us  [the longest x1 3.3 us: local(): pl.pallas_call(functools.partial(exchange_kernel, plan, shared, count), o...]
  transfers between devices with their start and end apart: 6 -> 6, of which waited for: 1 -> 1; matrix products, arithmetic and copies ran while one was open for 0% -> 0% of each run, Pallas kernels for 14% -> 15%
where the time goes in v1:
time: 15.1 us
  starting transfers between devices  8.38 us (55%)
  Pallas kernels  5.61 us (37%)
  waiting for transfers between devices  1.02 us (7%)
    ppermute x4, starting transfers between devices, between_blocks(): return lax.ppermute(block, AXES, pairs)  6.24 us
    pallas_call x1, Pallas kernels, local(): pl.pallas_call(functools.partial(exchange_kernel, plan, shared, count), o...  3.3 us
    pallas_call x1, Pallas kernels, local(): pl.pallas_call(stage_kernel, out_shape=(jax.ShapeDtypeStruct(density.shap...  2.3 us
    ppermute x2, starting transfers between devices, swap_cores(): return lax.ppermute(block, 'atoms', [(0, 1), (1, 0)])  2.15 us
    ppermute x2, waiting for transfers between devices, swap_cores(): return lax.ppermute(block, 'atoms', [(0, 1), (1, 0)])  1.01 us
  transfers between devices with their start and end apart: 6, of which 1 were waited for; matrix products, arithmetic and copies ran while one was open for 0% of the time, Pallas kernels for 15%

profile of v1, /device:TPU:1, one launch (start us, length us, event | category | flops | bytes accessed | tf_op | source)
XLA Modules:
  0.0 15.1 jit_solution(17861132920033198178)
XLA Ops:
  0.0 0.1 collective-permute-start.5
  0.1 3.7 %collective-permute-start.3 = (bf16[192,128]{1,0:T(8,128)(2,1)}, bf16[192,128]{1,0:T(8,128)(2,1)S(1)}, u32[]{:S(2)}, u32[]{:S(2)}) collective-permute-start(bf16[192,128]{1,0:T(8,128)(2,1)} %refs_0_.1), channel_id=1, source_target_pairs={{0,2},{2,6},{4,12},{6,10},{8,4},{10,14},{12,8},{14,0},{1,7},{3,11}... | collective-permute-start | bytes 147464 | tf_op jit(solution)/shard_map/ppermute | solution.py:18
  3.8 1.1 %collective-permute-start.2 = (bf16[192,128]{1,0:T(8,128)(2,1)}, bf16[192,128]{1,0:T(8,128)(2,1)S(1)}, u32[]{:S(2)}, u32[]{:S(2)}) collective-permute-start(bf16[192,128]{1,0:T(8,128)(2,1)} %refs_0_.1), channel_id=1, source_target_pairs={{0,8},{2,14},{4,10},{6,0},{8,12},{10,6},{12,2},{14,4},{1,13},{3,5}... | collective-permute-start | bytes 147464 | tf_op jit(solution)/shard_map/ppermute | solution.py:18
  4.8 1.2 %collective-permute-start.1 = (bf16[192,128]{1,0:T(8,128)(2,1)}, bf16[192,128]{1,0:T(8,128)(2,1)S(1)}, u32[]{:S(2)}, u32[]{:S(2)}) collective-permute-start(bf16[192,128]{1,0:T(8,128)(2,1)} %refs_0_.1), channel_id=1, source_target_pairs={{0,10},{2,12},{4,8},{6,14},{8,6},{10,0},{12,4},{14,2},{1,15},{3,9}... | collective-permute-start | bytes 147464 | tf_op jit(solution)/shard_map/ppermute | solution.py:18
  6.1 0.2 %collective-permute-start = (bf16[192,128]{1,0:T(8,128)(2,1)}, bf16[192,128]{1,0:T(8,128)(2,1)S(1)}, u32[]{:S(2)}, u32[]{:S(2)}) collective-permute-start(bf16[192,128]{1,0:T(8,128)(2,1)} %refs_0_.1), channel_id=1, source_target_pairs={{0,4},{2,0},{4,6},{6,2},{8,10},{10,8},{12,14},{14,12},{1,5},{3,1},... | collective-permute-start | bytes 147464 | tf_op jit(solution)/shard_map/ppermute | solution.py:18
  6.3 2.3 %shard_map.64 = (bf16[192,128]{1,0:T(8,128)(2,1)S(1)}, bf16[4,128,2048]{2,1,0:T(8,128)(2,1)S(1)}, bf16[1024,1024]{1,0:T(8,128)(2,1)S(1)}, bf16[16,128]{1,0:T(8,128)(2,1)S(1)}, s32[8,128]{1,0:T(8,128)S(1)}) custom-call(bf16[192,128]{1,0:T(8,128)(2,1)} %refs_0_.1, bf16[1,1,4,128,2048]{4,3,2,1,0:T(8,128)(2,1)} %refs_1_.1, bf16[1,1,1024,1024]{3,2,1,0:T(8,128)(2,1)} %refs_2_.1, ...), custom_call_target="tpu_custom_call" | custom-call | tf_op jit(solution)/shard_map/pallas_call | solution.py:171
  8.6 0.0 collective-permute-done.3
  8.6 0.0 collective-permute-done.2
  8.6 0.0 collective-permute-done.1
  8.7 2.1 %collective-permute-start.4 = (bf16[592,128]{1,0:T(8,128)(2,1)S(1)}, bf16[592,128]{1,0:T(8,128)(2,1)S(1)}, u32[]{:S(2)}, u32[]{:S(2)}) collective-permute-start(bf16[592,128]{1,0:T(8,128)(2,1)S(1)} %constant_dynamic-update-slice_fusion.packed), channel_id=1, source_target_pairs={{0,1},{1,0},{2,3},{3,2},{4,5},{5,4},{6,7},{7,6},{8,9},{9,8},{10,11... | collective-permute-start | bytes 454664 | tf_op jit(solution)/shard_map/ppermute | solution.py:22
  10.8 0.0 collective-permute-done.given
  10.8 1.0 %collective-permute-done.4.swapped = bf16[592,128]{1,0:T(8,128)(2,1)S(1)} collective-permute-done((bf16[592,128]{1,0:T(8,128)(2,1)S(1)}, bf16[592,128]{1,0:T(8,128)(2,1)S(1)}, u32[]{:S(2)}, u32[]{:S(2)}) %collective-permute-start.4) | collective-permute-done | bytes 151584 | tf_op jit(solution)/shard_map/ppermute | solution.py:22
  11.8 0.0 collective-permute-done.5.rows_other
  11.8 3.3 %shard_map.66 = f32[1,1,192,192]{3,2,1,0:T(8,128)} custom-call(bf16[192,128]{1,0:T(8,128)(2,1)S(1)} %get-tuple-element.17.own, bf16[192,128]{1,0:T(8,128)(2,1)S(1)} %shard_map.65.last, bf16[592,128]{1,0:T(8,128)(2,1)S(1)} %constant_dynamic-update-slice_fusion.packed, bf16[592,128]{1,0:T(8,128)(2,1)S(1)} %collective-permute-done.4.swapped, ...), custom_call_target="tpu_custom_call" | custom-call | tf_op jit(solution)/shard_map/pallas_call | solution.py:203
  (5 shorter events, 0.0 us)
Async XLA Ops:
  0.0 11.8 %collective-permute-start.5 = (bf16[1,1,4,128,2048]{4,3,2,1,0:T(8,128)(2,1)}, bf16[1,1,4,128,2048]{4,3,2,1,0:T(8,128)(2,1)S(1)}, u32[]{:S(2)}, u32[]{:S(2)}) collective-permute-start(bf16[1,1,4,128,2048]{4,3,2,1,0:T(8,128)(2,1)} %refs_1_.1), channel_id=1, source_target_pairs={{0,1},{1,0},{2,3},{3,2},{4,5},{5,4},{6,7},{7,6},{8,9},{9,8},{10,11... | collective-permute-start | bytes 6291464 | tf_op jit(solution)/shard_map/ppermute | solution.py:22
  0.1 8.6 %collective-permute-start.3 = (bf16[192,128]{1,0:T(8,128)(2,1)}, bf16[192,128]{1,0:T(8,128)(2,1)S(1)}, u32[]{:S(2)}, u32[]{:S(2)}) collective-permute-start(bf16[192,128]{1,0:T(8,128)(2,1)} %refs_0_.1), channel_id=1, source_target_pairs={{0,2},{2,6},{4,12},{6,10},{8,4},{10,14},{12,8},{14,0},{1,7},{3,11}... | collective-permute-start | bytes 147464 | tf_op jit(solution)/shard_map/ppermute | solution.py:18
  3.8 4.9 %collective-permute-start.2 = (bf16[192,128]{1,0:T(8,128)(2,1)}, bf16[192,128]{1,0:T(8,128)(2,1)S(1)}, u32[]{:S(2)}, u32[]{:S(2)}) collective-permute-start(bf16[192,128]{1,0:T(8,128)(2,1)} %refs_0_.1), channel_id=1, source_target_pairs={{0,8},{2,14},{4,10},{6,0},{8,12},{10,6},{12,2},{14,4},{1,13},{3,5}... | collective-permute-start | bytes 147464 | tf_op jit(solution)/shard_map/ppermute | solution.py:18
  4.8 3.8 %collective-permute-start.1 = (bf16[192,128]{1,0:T(8,128)(2,1)}, bf16[192,128]{1,0:T(8,128)(2,1)S(1)}, u32[]{:S(2)}, u32[]{:S(2)}) collective-permute-start(bf16[192,128]{1,0:T(8,128)(2,1)} %refs_0_.1), channel_id=1, source_target_pairs={{0,10},{2,12},{4,8},{6,14},{8,6},{10,0},{12,4},{14,2},{1,15},{3,9}... | collective-permute-start | bytes 147464 | tf_op jit(solution)/shard_map/ppermute | solution.py:18
  6.1 4.7 %collective-permute-start = (bf16[192,128]{1,0:T(8,128)(2,1)}, bf16[192,128]{1,0:T(8,128)(2,1)S(1)}, u32[]{:S(2)}, u32[]{:S(2)}) collective-permute-start(bf16[192,128]{1,0:T(8,128)(2,1)} %refs_0_.1), channel_id=1, source_target_pairs={{0,4},{2,0},{4,6},{6,2},{8,10},{10,8},{12,14},{14,12},{1,5},{3,1},... | collective-permute-start | bytes 147464 | tf_op jit(solution)/shard_map/ppermute | solution.py:18
  8.7 3.1 %collective-permute-start.4 = (bf16[592,128]{1,0:T(8,128)(2,1)S(1)}, bf16[592,128]{1,0:T(8,128)(2,1)S(1)}, u32[]{:S(2)}, u32[]{:S(2)}) collective-permute-start(bf16[592,128]{1,0:T(8,128)(2,1)S(1)} %constant_dynamic-update-slice_fusion.packed), channel_id=1, source_target_pairs={{0,1},{1,0},{2,3},{3,2},{4,5},{5,4},{6,7},{7,6},{8,9},{9,8},{10,11... | collective-permute-start | bytes 454664 | tf_op jit(solution)/shard_map/ppermute | solution.py:22

commit v2 on v1

--- a/solution.py
+++ b/solution.py
@@ -27,8 +27,8 @@
 
 
 EIGHT = (
-    ((1, 3, 6, 5, 2, 7, 4, 0), (4, 7, 5, 0, 6, 3, 1, 2), (5, 6, 4, 7, 3, 0, 2, 1), (2, 0, 3, 1, 5, 4, 7, 6)),
-    ((3, 5, 1, 6, 7, 2, 0, 4), (6, 2, 7, 4, 0, 1, 3, 5), (7, 4, 0, 2, 1, 6, 5, 3), (2, 0, 3, 1, 5, 4, 7, 6)),
+    ((1, 3, 4, 5, 2, 7, 0, 6), (6, 5, 1, 7, 0, 3, 2, 4), (7, 4, 0, 1, 6, 2, 5, 3), (2, 0, 3, 6, 7, 1, 4, 5)),
+    ((3, 6, 7, 4, 5, 0, 1, 2), (4, 7, 5, 2, 1, 6, 3, 0), (5, 2, 6, 0, 3, 4, 7, 1), (2, 0, 3, 6, 7, 1, 4, 5)),
 )
 
 

time: 15.1 us -> 14.5 us (0.960)
  the two profiles are of different devices: /device:TPU:1 before, /device:TPU:0 now
where the time goes in v2:
time: 14.5 us; the launch traced here: 14.6 us
  starting transfers between devices  7.75 us (53%)
  Pallas kernels  5.61 us (39%)
  waiting for transfers between devices  1.19 us (8%)
    ppermute x4, starting transfers between devices, between_blocks(): return lax.ppermute(block, AXES, pairs)  6.68 us
    pallas_call x1, Pallas kernels, local(): pl.pallas_call(functools.partial(exchange_kernel, plan, shared, count), o...  3.3 us
    pallas_call x1, Pallas kernels, local(): pl.pallas_call(stage_kernel, out_shape=(jax.ShapeDtypeStruct(density.shap...  2.3 us
    ppermute x4, waiting for transfers between devices, between_blocks(): return lax.ppermute(block, AXES, pairs)  1.19 us
    ppermute x2, starting transfers between devices, swap_cores(): return lax.ppermute(block, 'atoms', [(0, 1), (1, 0)])  1.07 us
  transfers between devices with their start and end apart: 6, of which 2 were waited for; matrix products, arithmetic and copies ran while one was open for 0% of the time, Pallas kernels for 16%

profile of v2, /device:TPU:0, one launch (start us, length us, event | category | flops | bytes accessed | tf_op | source)
XLA Modules:
  0.0 14.6 jit_solution(10730253428188373257)
XLA Ops:
  0.0 0.5 %collective-permute-start.5 = (bf16[1,1,4,128,2048]{4,3,2,1,0:T(8,128)(2,1)}, bf16[1,1,4,128,2048]{4,3,2,1,0:T(8,128)(2,1)S(1)}, u32[]{:S(2)}, u32[]{:S(2)}) collective-permute-start(bf16[1,1,4,128,2048]{4,3,2,1,0:T(8,128)(2,1)} %refs_1_.1), channel_id=1, source_target_pairs={{0,1},{1,0},{2,3},{3,2},{4,5},{5,4},{6,7},{7,6},{8,9},{9,8},{10,11... | collective-permute-start | bytes 6291464 | tf_op jit(solution)/shard_map/ppermute | solution.py:22
  0.5 2.5 %collective-permute-start.3 = (bf16[192,128]{1,0:T(8,128)(2,1)}, bf16[192,128]{1,0:T(8,128)(2,1)S(1)}, u32[]{:S(2)}, u32[]{:S(2)}) collective-permute-start(bf16[192,128]{1,0:T(8,128)(2,1)} %refs_0_.1), channel_id=1, source_target_pairs={{0,2},{2,6},{4,8},{6,10},{8,4},{10,14},{12,0},{14,12},{1,7},{3,13}... | collective-permute-start | bytes 147464 | tf_op jit(solution)/shard_map/ppermute | solution.py:18
  3.0 2.1 %collective-permute-start.2 = (bf16[192,128]{1,0:T(8,128)(2,1)}, bf16[192,128]{1,0:T(8,128)(2,1)S(1)}, u32[]{:S(2)}, u32[]{:S(2)}) collective-permute-start(bf16[192,128]{1,0:T(8,128)(2,1)} %refs_0_.1), channel_id=1, source_target_pairs={{0,12},{2,10},{4,2},{6,14},{8,0},{10,6},{12,4},{14,8},{1,9},{3,15}... | collective-permute-start | bytes 147464 | tf_op jit(solution)/shard_map/ppermute | solution.py:18
  5.1 1.7 %collective-permute-start.1 = (bf16[192,128]{1,0:T(8,128)(2,1)}, bf16[192,128]{1,0:T(8,128)(2,1)S(1)}, u32[]{:S(2)}, u32[]{:S(2)}) collective-permute-start(bf16[192,128]{1,0:T(8,128)(2,1)} %refs_0_.1), channel_id=1, source_target_pairs={{0,14},{2,8},{4,0},{6,2},{8,12},{10,4},{12,10},{14,6},{1,11},{3,5}... | collective-permute-start | bytes 147464 | tf_op jit(solution)/shard_map/ppermute | solution.py:18
  6.9 0.3 %collective-permute-start = (bf16[192,128]{1,0:T(8,128)(2,1)}, bf16[192,128]{1,0:T(8,128)(2,1)S(1)}, u32[]{:S(2)}, u32[]{:S(2)}) collective-permute-start(bf16[192,128]{1,0:T(8,128)(2,1)} %refs_0_.1), channel_id=1, source_target_pairs={{0,4},{2,0},{4,6},{6,12},{8,14},{10,2},{12,8},{14,10},{1,5},{3,1},... | collective-permute-start | bytes 147464 | tf_op jit(solution)/shard_map/ppermute | solution.py:18
  7.1 2.3 %shard_map.64 = (bf16[192,128]{1,0:T(8,128)(2,1)S(1)}, bf16[4,128,2048]{2,1,0:T(8,128)(2,1)S(1)}, bf16[1024,1024]{1,0:T(8,128)(2,1)S(1)}, bf16[16,128]{1,0:T(8,128)(2,1)S(1)}, s32[8,128]{1,0:T(8,128)S(1)}) custom-call(bf16[192,128]{1,0:T(8,128)(2,1)} %refs_0_.1, bf16[1,1,4,128,2048]{4,3,2,1,0:T(8,128)(2,1)} %refs_1_.1, bf16[1,1,1024,1024]{3,2,1,0:T(8,128)(2,1)} %refs_2_.1, ...), custom_call_target="tpu_custom_call" | custom-call | tf_op jit(solution)/shard_map/pallas_call | solution.py:171
  9.4 0.0 collective-permute-done.3
  9.5 0.0 collective-permute-done.2
  9.5 0.2 %collective-permute-done.1 = bf16[192,128]{1,0:T(8,128)(2,1)S(1)} collective-permute-done((bf16[192,128]{1,0:T(8,128)(2,1)}, bf16[192,128]{1,0:T(8,128)(2,1)S(1)}, u32[]{:S(2)}, u32[]{:S(2)}) %collective-permute-start.1) | collective-permute-done | bytes 49184 | tf_op jit(solution)/shard_map/ppermute | solution.py:18
  9.7 0.6 %collective-permute-start.4 = (bf16[592,128]{1,0:T(8,128)(2,1)S(1)}, bf16[592,128]{1,0:T(8,128)(2,1)S(1)}, u32[]{:S(2)}, u32[]{:S(2)}) collective-permute-start(bf16[592,128]{1,0:T(8,128)(2,1)S(1)} %constant_dynamic-update-slice_fusion.packed), channel_id=1, source_target_pairs={{0,1},{1,0},{2,3},{3,2},{4,5},{5,4},{6,7},{7,6},{8,9},{9,8},{10,11... | collective-permute-start | bytes 454664 | tf_op jit(solution)/shard_map/ppermute | solution.py:22
  10.3 1.0 %collective-permute-done.given = bf16[192,128]{1,0:T(8,128)(2,1)S(1)} collective-permute-done((bf16[192,128]{1,0:T(8,128)(2,1)}, bf16[192,128]{1,0:T(8,128)(2,1)S(1)}, u32[]{:S(2)}, u32[]{:S(2)}) %collective-permute-start) | collective-permute-done | bytes 49184 | tf_op jit(solution)/shard_map/ppermute | solution.py:18
  11.3 0.0 collective-permute-done.4.swapped
  11.3 0.0 collective-permute-done.5.rows_other
  11.3 3.3 %shard_map.66 = f32[1,1,192,192]{3,2,1,0:T(8,128)} custom-call(bf16[192,128]{1,0:T(8,128)(2,1)S(1)} %get-tuple-element.17.own, bf16[192,128]{1,0:T(8,128)(2,1)S(1)} %shard_map.65.last, bf16[592,128]{1,0:T(8,128)(2,1)S(1)} %constant_dynamic-update-slice_fusion.packed, bf16[592,128]{1,0:T(8,128)(2,1)S(1)} %collective-permute-done.4.swapped, ...), custom_call_target="tpu_custom_call" | custom-call | tf_op jit(solution)/shard_map/pallas_call | solution.py:203
  (5 shorter events, 0.0 us)
Async XLA Ops:
  0.0 11.3 %collective-permute-start.5 = (bf16[1,1,4,128,2048]{4,3,2,1,0:T(8,128)(2,1)}, bf16[1,1,4,128,2048]{4,3,2,1,0:T(8,128)(2,1)S(1)}, u32[]{:S(2)}, u32[]{:S(2)}) collective-permute-start(bf16[1,1,4,128,2048]{4,3,2,1,0:T(8,128)(2,1)} %refs_1_.1), channel_id=1, source_target_pairs={{0,1},{1,0},{2,3},{3,2},{4,5},{5,4},{6,7},{7,6},{8,9},{9,8},{10,11... | collective-permute-start | bytes 6291464 | tf_op jit(solution)/shard_map/ppermute | solution.py:22
  0.5 9.0 %collective-permute-start.3 = (bf16[192,128]{1,0:T(8,128)(2,1)}, bf16[192,128]{1,0:T(8,128)(2,1)S(1)}, u32[]{:S(2)}, u32[]{:S(2)}) collective-permute-start(bf16[192,128]{1,0:T(8,128)(2,1)} %refs_0_.1), channel_id=1, source_target_pairs={{0,2},{2,6},{4,8},{6,10},{8,4},{10,14},{12,0},{14,12},{1,7},{3,13}... | collective-permute-start | bytes 147464 | tf_op jit(solution)/shard_map/ppermute | solution.py:18
  3.0 6.5 %collective-permute-start.2 = (bf16[192,128]{1,0:T(8,128)(2,1)}, bf16[192,128]{1,0:T(8,128)(2,1)S(1)}, u32[]{:S(2)}, u32[]{:S(2)}) collective-permute-start(bf16[192,128]{1,0:T(8,128)(2,1)} %refs_0_.1), channel_id=1, source_target_pairs={{0,12},{2,10},{4,2},{6,14},{8,0},{10,6},{12,4},{14,8},{1,9},{3,15}... | collective-permute-start | bytes 147464 | tf_op jit(solution)/shard_map/ppermute | solution.py:18
  5.1 4.5 %collective-permute-start.1 = (bf16[192,128]{1,0:T(8,128)(2,1)}, bf16[192,128]{1,0:T(8,128)(2,1)S(1)}, u32[]{:S(2)}, u32[]{:S(2)}) collective-permute-start(bf16[192,128]{1,0:T(8,128)(2,1)} %refs_0_.1), channel_id=1, source_target_pairs={{0,14},{2,8},{4,0},{6,2},{8,12},{10,4},{12,10},{14,6},{1,11},{3,5}... | collective-permute-start | bytes 147464 | tf_op jit(solution)/shard_map/ppermute | solution.py:18
  6.9 4.5 %collective-permute-start = (bf16[192,128]{1,0:T(8,128)(2,1)}, bf16[192,128]{1,0:T(8,128)(2,1)S(1)}, u32[]{:S(2)}, u32[]{:S(2)}) collective-permute-start(bf16[192,128]{1,0:T(8,128)(2,1)} %refs_0_.1), channel_id=1, source_target_pairs={{0,4},{2,0},{4,6},{6,12},{8,14},{10,2},{12,8},{14,10},{1,5},{3,1},... | collective-permute-start | bytes 147464 | tf_op jit(solution)/shard_map/ppermute | solution.py:18
  9.7 1.7 %collective-permute-start.4 = (bf16[592,128]{1,0:T(8,128)(2,1)S(1)}, bf16[592,128]{1,0:T(8,128)(2,1)S(1)}, u32[]{:S(2)}, u32[]{:S(2)}) collective-permute-start(bf16[592,128]{1,0:T(8,128)(2,1)S(1)} %constant_dynamic-update-slice_fusion.packed), channel_id=1, source_target_pairs={{0,1},{1,0},{2,3},{3,2},{4,5},{5,4},{6,7},{7,6},{8,9},{9,8},{10,11... | collective-permute-start | bytes 454664 | tf_op jit(solution)/shard_map/ppermute | solution.py:22
